TPU v7x, 512 devices: a whole 4x8x8 slice. The times are simulated.
512 devices in a mesh: chan: 32 (over y_hi, z), tm: 16 (over y_lo, x, core).
Axes of the slice: x: 4, y: 8 (y_hi: 4, y_lo: 2; y = y_hi * 2 + y_lo), z: 8, core: 2. Of those that a mesh axis runs over, the one named last changes fastest.
Arguments:
- strain_record: bfloat16 [4096, 131072], P('chan', 'tm')
- dead_channels: int32 [200], replicated, may hold values from 1 to 4094, as said below
- source_channels: int32 [1024], P('chan'), may hold values from 0 to 4095, as said below
- band_start: int32 [1], replicated, may hold values from 1 to 176
Outputs:
- cross_spectra: bfloat16 [2, 80, 1024, 4096], P(None, 'tm', None, 'chan')
Inputs may be any that keep to these rules, and one draw needn't show every extreme that they name: `dead_channels`: distinct channel indices. `source_channels`: each block of 128 consecutive channels holds exactly 32 sources, in increasing order; entry s lies in block s // 32.
All inputs are finite; a program needn't handle non-finite values.
Results may differ from a plain program's by a relative error of at most 0.0056.
Values may be sent and summed in bfloat16 or wider, within the bound.
A program may use at most 64 MiB of HBM per device.

v0:
```python
import jax
import jax.numpy as jnp
from jax import lax
from jax.sharding import PartitionSpec as P

NFFT = 512
FQ_DEV = 5


EPS = 1e-06


def make_table(band_start, nbins):
    n_int = jnp.arange(NFFT, dtype=jnp.int32)
    k_int = band_start[0] + jnp.arange(nbins, dtype=jnp.int32)
    phase_idx = k_int[:, None] * n_int[None, :] % NFFT
    angle_val = 2.0 * jnp.pi / NFFT * phase_idx.astype(jnp.float32)
    taper_val = 0.5 - 0.5 * jnp.cos(2.0 * jnp.pi / NFFT * n_int.astype(jnp.float32))
    cos_part = taper_val[None, :] * jnp.cos(angle_val)
    sin_part = -taper_val[None, :] * jnp.sin(angle_val)
    return jnp.concatenate([cos_part, sin_part], axis=0).astype(jnp.bfloat16)


def body(strain_record, dead_channels, source_channels, band_start):
    chan_dev = strain_record.shape[0]
    blk_dev = strain_record.shape[1] // NFFT
    n_time = lax.axis_size("tm")
    nbins = FQ_DEV * n_time
    first_chan = lax.axis_index("chan") * chan_dev
    chan_ids = first_chan + jnp.arange(chan_dev, dtype=jnp.int32)
    live_mask = 1.0 - jnp.any(chan_ids[:, None] == dead_channels[None, :], axis=1).astype(
        jnp.float32
    )
    live_count = chan_dev * lax.axis_size("chan") - dead_channels.shape[0]
    dft_table = make_table(band_start, nbins)
    time_blocks = strain_record.reshape(chan_dev, blk_dev, NFFT)
    raw_spec = lax.dot_general(
        dft_table, time_blocks, (((1,), (2,)), ((), ())), preferred_element_type=jnp.float32
    ).reshape(2, nbins, chan_dev, blk_dev)
    sample_sums = jnp.dot(
        live_mask.astype(jnp.bfloat16), strain_record, preferred_element_type=jnp.float32
    )
    mean_trace = lax.psum(sample_sums, "chan") / live_count
    common_mode = lax.dot_general(
        dft_table.astype(jnp.float32),
        mean_trace.reshape(blk_dev, NFFT),
        (((1,), (1,)), ((), ())),
        precision=lax.Precision.HIGHEST,
    ).reshape(2, nbins, blk_dev)
    spectra = (live_mask[None, None, :, None] * (raw_spec - common_mode[:, :, None, :])).astype(
        jnp.bfloat16
    )
    band_spec = lax.all_to_all(spectra, "tm", split_axis=1, concat_axis=3, tiled=True)
    fq_dev = band_spec.shape[1]
    blocks = band_spec.shape[3]
    spec_full = band_spec.astype(jnp.float32)
    power = jnp.sum(spec_full * spec_full, axis=(0, 3)) / blocks
    whitened = (spec_full * lax.rsqrt(power + EPS)[None, :, :, None]).astype(jnp.bfloat16)
    src_dev = source_channels.shape[0]
    offsets = source_channels - first_chan
    selector = (offsets[:, None] == jnp.arange(chan_dev, dtype=jnp.int32)[None, :]).astype(
        jnp.bfloat16
    )
    source_rows = jnp.einsum(
        "sc,pkcb->spkb", selector, whitened, preferred_element_type=jnp.float32
    ).astype(jnp.bfloat16)
    source_rows = source_rows.reshape(src_dev, 2 * fq_dev * blocks)
    white_real = whitened[0]
    white_imag = whitened[1]

    def mult(left, right):
        return jnp.einsum("skb,kcb->ksc", left, right, preferred_element_type=jnp.float32)

    rows_piece = lax.all_gather(source_rows, "chan", axis=0, tiled=True)
    count_rows = rows_piece.shape[0]
    shaped = rows_piece.reshape(count_rows, 2, fq_dev, blocks)
    src_real = shaped[:, 0]
    src_imag = shaped[:, 1]
    real_part = mult(src_real, white_real) + mult(src_imag, white_imag)
    imag_part = mult(src_real, white_imag) - mult(src_imag, white_real)
    return (jnp.stack([real_part, imag_part]) / blocks).astype(jnp.bfloat16)


def solution(mesh):
    in_specs = (P("chan", "tm"), P(), P("chan"), P())
    out_specs = P(None, "tm", None, "chan")
    return jax.shard_map(body, mesh=mesh, in_specs=in_specs, out_specs=out_specs, check_vma=False)
```

profile of v0, /device:TPU:8, one launch (start us, length us, event | category | flops | bytes accessed | tf_op | source)
XLA Modules:
  0.0 323.2 jit_solution(2446822868380168388)
XLA Ops:
  6.5 0.0 copy-start.1
  7.4 0.8 compare_reduce_fusion
  8.2 2.0 fusion.20
  10.2 164.0 %psum.7 = f32[8192]{0:T(1024)S(1)} all-reduce(f32[8192]{0:T(1024)S(1)} %bitcast.82), channel_id=1, replica_groups=mesh['chan'=32,'tm'=16] {'chan'}, use_global_device_ids=true, to_apply=%region_1.2 | all-reduce | flops 8192 | bytes 65536 | tf_op jit(solution)/shard_map/psum | solution.py:43
  174.1 0.7 multiply_convert_fusion.2
  174.9 0.3 fusion.23
  175.2 0.0 copy-done.1
  175.2 0.0 copy-start.2
  175.2 0.9 fusion.9
  176.1 1.0 copy.25
  177.1 5.8 %all-to-all-start = ((bf16[2,80,128,16]{2,3,0,1:T(8,128)(2,1)}), bf16[2,80,128,16]{2,3,0,1:T(8,128)(2,1)S(1)}, u32[]{:S(2)}, u32[]{:S(2)}) async-start(bf16[2,80,128,16]{2,3,0,1:T(8,128)(2,1)} %copy.25), calls=%async_computation | async-start | bytes 1310720 | tf_op jit(solution)/shard_map/all_to_all | solution.py:53
  182.9 0.0 all-gather.2.cloned.1.call-start
  182.9 0.0 copy-done.2
  182.9 10.8 %all-to-all-done = bf16[2,80,128,16]{2,3,0,1:T(8,128)(2,1)S(1)} async-done(((bf16[2,80,128,16]{2,3,0,1:T(8,128)(2,1)}), bf16[2,80,128,16]{2,3,0,1:T(8,128)(2,1)S(1)}, u32[]{:S(2)}, u32[]{:S(2)}) %all-to-all-start) | async-done | bytes 655392 | tf_op jit(solution)/shard_map/all_to_all | solution.py:53
  193.8 0.2 multiply_reduce_fusion
  194.0 0.1 copy_convert_fusion
  194.1 0.1 copy.27
  194.2 0.4 copy.28
  194.6 0.2 multiply_convert_fusion
  194.8 0.3 convolution_convert_fusion
  195.1 0.1 copy.29
  195.2 0.9 reshape.74
  196.0 0.0 all-gather.2.cloned.1.call-update
  196.1 103.8 %all-gather.2.cloned.1.call-done = bf16[1024,2560]{1,0:T(8,128)(2,1)} async-done(((bf16[32,2560]{1,0:T(8,128)(2,1)}), bf16[1024,2560]{1,0:T(8,128)(2,1)}) %all-gather.2.cloned.1.call-update) | async-done | bytes 5242896 | tf_op jit(solution)/shard_map/all_gather | solution.py:74
  299.9 7.9 %copy.30 = bf16[1024,2560]{0,1:T(8,128)(2,1)} copy(bf16[1024,2560]{1,0:T(8,128)(2,1)} %all-gather.2.cloned.1.call-done) | data formatting | bytes 10485760 | tf_op jit(solution)/shard_map/all_gather | solution.py:74
  307.8 0.0 copy-start
  307.8 2.9 fusion.1
  310.8 0.3 copy-done
  311.1 1.1 fusion.2
  312.2 1.1 subtract_bitcast_fusion
  313.2 1.1 add_bitcast_fusion
  314.3 2.1 fusion
  (11 shorter events, 0.1 us)
Async XLA Ops:
  6.5 168.6 %copy-start.1 = (bf16[128,8192]{1,0:T(8,128)(2,1)S(1)}, bf16[128,8192]{1,0:T(8,128)(2,1)}, u32[]{:S(2)}) copy-start(bf16[128,8192]{1,0:T(8,128)(2,1)} %param.4) | copy-start | bytes 6291460
  175.2 7.7 %copy-start.2 = (s32[32]{0:T(128)S(1)}, s32[32]{0:T(128)}, u32[]{:S(2)}) copy-start(s32[32]{0:T(128)} %param.6) | copy-start | bytes 388
  177.1 16.7 %all-to-all-start = ((bf16[2,80,128,16]{2,3,0,1:T(8,128)(2,1)}), bf16[2,80,128,16]{2,3,0,1:T(8,128)(2,1)S(1)}, u32[]{:S(2)}, u32[]{:S(2)}) async-start(bf16[2,80,128,16]{2,3,0,1:T(8,128)(2,1)} %copy.25), calls=%async_computation | async-start | bytes 1310720 | tf_op jit(solution)/shard_map/all_to_all | solution.py:53
  182.9 117.0 %all-gather.2.cloned.1.call-start = ((), (), s32[]{:S(2)}) async-start(), calls=%async_computation.1 | async-start | bytes 5406720 | tf_op jit(solution)/shard_map/all_gather | solution.py:74
  307.8 3.3 %copy-start = (bf16[1024,2560]{0,1:T(8,128)(2,1)S(1)}, bf16[1024,2560]{0,1:T(8,128)(2,1)}, u32[]{:S(2)}) copy-start(bf16[1024,2560]{0,1:T(8,128)(2,1)} %copy.30) | copy-start | bytes 15728644
Sparse Core Ops, SparseCore 0:
  196.2 103.6 all-gather.1
where the time goes:
time: 324 us; the launch traced here: 323 us
  blocking collectives  164 us (51%)
  waiting for transfers between devices  115 us (35%)
  between operations  14.4 us (4%)
  local copies, waits for them, and re-layouts  10.8 us (3%)
  matrix products  9.49 us (3%)
  starting transfers between devices  5.82 us (2%)
  other arithmetic  4.15 us (1%)
    psum x1, blocking collectives, body(): mean_trace = lax.psum(sample_sums, 'chan') / live_count  164 us
    all_gather x1, waiting for transfers between devices, body(): rows_piece = lax.all_gather(source_rows, 'chan', axis=0, tiled=True)  104 us
    all_to_all x1, waiting for transfers between devices, body(): lax.all_to_all(spectra, 'tm', split_axis=1, concat_axis=3, tiled=True)  10.8 us
    all_gather x1, local copies, waits for them, and re-layouts, body(): rows_piece = lax.all_gather(source_rows, 'chan', axis=0, tiled=True)  7.94 us
  transfers between devices with their start and end apart: 2, of which 2 were waited for; matrix products, arithmetic and copies ran while one was open for 0% of the time, Pallas kernels for 0%

commit v1 on v0

v1 whole, which is shorter than its diff:
```python
import jax
import jax.numpy as jnp
import numpy as np
from jax import lax
from jax.experimental import pallas as pl
from jax.experimental.pallas import tpu as pltpu
from jax.sharding import PartitionSpec as P

NFFT = 512
FQ = 5
NT = 16
NY, NZ = 4, 8
CH = 128
SRC = 32
HALF = 16
NCHAN = NY * NZ * CH
BLOCKS = 256
DEAD = 200
ROWS = 2 * FQ * NT
PAD = 256
EPS = 1e-06
NP1, NP2 = 7, 3

UNITS = {(0, 0): (2, 0), (0, 1): (1, 0), (1, 0): (2, 1), (1, 1): (1, 1), (2, 0): (2, 2), (2, 1): (1, 2), (3, 0): (1, 3), (3, 1): (1, 4), (4, 0): (1, 5), (4, 1): (1, 6)}
PLACE = {unit: at for at, unit in UNITS.items()}
EARLY = (0, 1, 2)
GROUPS = ((0, 1), (1, 3), (3, 5))
LATE = 4
TAKE, Y1, Z1, OWN1, Z2, Y2 = range(6)
ORDER = (
    (TAKE, 0, 0), (OWN1, 0, 0), (Y1, 0, 0), (Z2, 0, 0), (TAKE, 1, 0), (OWN1, 1, 0), (Y1, 1, 0), (Z2, 1, 0),
    (OWN1, 2, 0), (Y1, 2, 0), (Z2, 2, 0), (OWN1, 0, 1), (Y1, 0, 1), (Z2, 0, 1), (OWN1, 1, 1), (TAKE, 2, 0),
    (Y1, 3, 0), (Y1, 4, 0), (Y1, 5, 0), (Y1, 6, 0), (Y1, 1, 1), (Z2, 1, 1), (OWN1, 2, 1), (Y1, 2, 1), (Z2, 2, 1),
    (OWN1, 0, 2), (Z1, 0, 0), (Z2, 0, 2), (OWN1, 1, 2), (Z2, 1, 2), (Y1, 3, 1), (OWN1, 2, 2), (Z2, 2, 2),
    (Y1, 4, 1), (OWN1, 0, 3), (Y1, 5, 1), (Z1, 0, 1), (Y1, 6, 1), (Z2, 0, 3), (OWN1, 1, 3), (Z1, 1, 0), (Z1, 2, 0),
    (Z2, 1, 3), (OWN1, 2, 3), (Z1, 3, 0), (Z2, 2, 3), (Z1, 4, 0), (Z1, 5, 0), (Z1, 6, 0), (Z1, 0, 2), (Y2, 0, 0),
    (Z1, 1, 1), (Y2, 1, 0), (Z1, 2, 1), (Z1, 3, 1), (Y2, 2, 0), (Z1, 4, 1), (Z1, 5, 1), (Y2, 0, 1), (Z1, 6, 1),
    (Z1, 0, 3), (Z1, 1, 2), (Z1, 2, 2), (Z1, 3, 2), (Y2, 1, 1), (Z1, 4, 2), (Z1, 5, 2), (Z1, 6, 2), (Z1, 0, 4),
    (Z1, 1, 3), (Y2, 2, 1), (Z1, 2, 3), (Z1, 3, 3), (Y2, 0, 2), (Z1, 4, 3), (Z1, 5, 3), (Y2, 1, 2), (Z1, 6, 3),
    (Z1, 1, 4), (Z1, 2, 4), (Z1, 3, 4), (Y2, 2, 2), (Z1, 4, 4), (Z1, 5, 4), (Z1, 6, 4),
)


def fixed_tables():
    n = np.arange(NFFT)
    taper = 0.5 - 0.5 * np.cos(2.0 * np.pi / NFFT * n)
    bins = (np.arange(FQ)[:, None] + FQ * np.arange(NT)[None, :]).reshape(-1)
    angle = 2.0 * np.pi / NFFT * (bins[:, None] * n[None, :] % NFFT)
    return np.stack([taper * np.cos(angle), taper * np.sin(angle)]).astype(np.float32)


def dot_nt(left, right):
    return lax.dot_general(left, right, (((1,), (1,)), ((), ())), preferred_element_type=jnp.float32)


def kernel(
    x_hbm, fixed_hbm, dead_hbm, source_hbm, start_ref, out_ref,
    x_ref, fixed, dead_ref, source_ref, table_ref, sel_ref, spec, raw, sums,
    part, parts_in, line, lines_in, common, send, band, mats, g1, g2,
    in_sem, ps_send, ps_recv, re_send, re_recv, s1, r1, s2, r2,
):
    chan, tm = lax.axis_index("chan"), lax.axis_index("tm")
    y, z = chan // NZ, chan % NZ

    def at_y(step):
        return {"chan": (y + step + NY) % NY * NZ + z}

    def at_z(step):
        return {"chan": y * NZ + (z + step + NZ) % NZ}

    def at_t(step):
        return {"tm": (tm + step) % NT}

    def remote(src, dst, send_sem, recv_sem, where):
        return pltpu.make_async_remote_copy(
            src_ref=src, dst_ref=dst, send_sem=send_sem, recv_sem=recv_sem,
            device_id=where, device_id_type=pl.DeviceIdType.MESH,
        )

    sent = {}

    def start(key, *args):
        copy = remote(*args)
        copy.start()
        sent.setdefault(key, []).append(copy)

    def settle(key):
        for copy in sent.pop(key, []):
            copy.wait_send()

    def arrived(ref, sem):
        pltpu.make_async_copy(ref, ref, sem).wait()

    fetches = [
        pltpu.make_async_copy(dead_hbm, dead_ref, in_sem.at[0]),
        pltpu.make_async_copy(source_hbm, source_ref, in_sem.at[1]),
        pltpu.make_async_copy(fixed_hbm, fixed, in_sem.at[2]),
    ]
    quarter = NT * NFFT // 4
    for k in range(4):
        part_of = slice(k * quarter, (k + 1) * quarter)
        fetches.append(pltpu.make_async_copy(x_hbm.at[:, part_of], x_ref.at[:, part_of], in_sem.at[3 + k]))
    for fetch in fetches:
        fetch.start()

    barrier = pltpu.get_barrier_semaphore()
    for peer in (
        [at_z(s) for s in range(1, NZ)] + [at_y(s) for s in range(1, NY)] + [at_t(s) for s in range(1, NT)]
    ):
        pl.semaphore_signal(barrier, inc=1, device_id=peer, device_id_type=pl.DeviceIdType.MESH)

    for k in range(2):
        fetches[k].wait()
    phase = start_ref[0] * lax.broadcasted_iota(jnp.int32, (8, NFFT), 1) % NFFT
    angle = 2.0 * jnp.pi / NFFT * phase.astype(jnp.float32)
    shift_cos = jnp.concatenate([jnp.cos(angle)] * 2, axis=0)
    shift_sin = jnp.concatenate([jnp.sin(angle)] * 2, axis=0)
    ids = chan * CH + lax.broadcasted_iota(jnp.int32, (8, CH), 1)

    def strike(step, mask):
        for k in range(8):
            mask = jnp.where(ids == dead_ref[8 * step + k], 0.0, mask)
        return mask

    live = lax.fori_loop(0, DEAD // 8, strike, jnp.ones((8, CH), jnp.float32))
    live_rows = jnp.broadcast_to(live[0:1], (CH, CH)).T
    live_rows = jnp.concatenate([live_rows, live_rows], axis=1)
    source_ids = chan * CH + lax.broadcasted_iota(jnp.int32, (SRC, CH), 1)
    source_rows = lax.broadcasted_iota(jnp.int32, (SRC, CH), 0)
    wanted = jnp.zeros((SRC, CH), jnp.int32)
    for k in range(SRC):
        wanted = jnp.where(source_rows == k, source_ref[k], wanted)
    sel_ref[...] = jnp.where(wanted == source_ids, 1.0, 0.0).astype(jnp.bfloat16)
    fetches[2].wait()
    for i in range(FQ):
        cos_i, sin_i = fixed[0, NT * i:NT * (i + 1)], fixed[1, NT * i:NT * (i + 1)]
        table_ref[32 * i:32 * i + 16] = (shift_cos * cos_i - shift_sin * sin_i).astype(jnp.bfloat16)
        table_ref[32 * i + 16:32 * i + 32] = (-(shift_sin * cos_i + shift_cos * sin_i)).astype(jnp.bfloat16)
    table_ref[ROWS:] = jnp.zeros((PAD - ROWS, NFFT), jnp.bfloat16)

    for k in range(4):
        fetches[3 + k].wait()
        blocks = [x_ref[:, (4 * k + b) * NFFT:(4 * k + b + 1) * NFFT] for b in range(4)]
        values = dot_nt(jnp.concatenate(blocks, axis=0), table_ref[...])
        for b in range(4):
            value = values[CH * b:CH * (b + 1)]
            spec[4 * k + b] = value
            sums[4 * k + b:4 * k + b + 1] = jnp.sum(value * live_rows, axis=0, keepdims=True)
    for q in range(3):
        lanes = slice(64 * q, 64 * q + 64)
        part[q] = jnp.concatenate([sums[0:8, lanes], sums[8:16, lanes]], axis=1)

    pl.semaphore_wait(barrier, (NZ - 1) + (NY - 1) + (NT - 1))

    pieces = (slice(0, 1), slice(1, 3))
    for n, piece in enumerate(pieces):
        for s in range(1, NZ):
            start(
                "sum", part.at[piece], parts_in.at[s - 1, piece],
                ps_send.at[n, s - 1], ps_recv.at[n, s - 1], at_z(s),
            )

    def turn(b, carry):
        to = pl.multiple_of(b * ROWS, ROWS)
        raw[pl.ds(to, CH), :] = spec[b, :, 0:CH].T
        raw[pl.ds(to + CH, ROWS - CH), :] = spec[b, :, CH:].T[0:ROWS - CH]
        return carry

    lax.fori_loop(0, NT // 2, turn, 0)
    for n, piece in enumerate(pieces):
        total = part[piece]
        for s in range(1, NZ):
            arrived(parts_in.at[s - 1, piece], ps_recv.at[n, s - 1])
            total = total + parts_in[s - 1, piece]
        line[piece] = total
        for s in range(1, NY):
            start(
                "sum", line.at[piece], lines_in.at[s - 1, piece],
                ps_send.at[n, 6 + s], ps_recv.at[n, 6 + s], at_y(s),
            )
    lax.fori_loop(NT // 2, NT, turn, 0)

    def close_sum(n):
        piece = pieces[n]
        total = line[piece]
        for s in range(1, NY):
            arrived(lines_in.at[s - 1, piece], ps_recv.at[n, 6 + s])
            total = total + lines_in[s - 1, piece]
        common[piece] = total / (NCHAN - DEAD)

    def give(group):
        first, last = GROUPS[group]
        for i in range(first, last):
            mode = common[i // 2]
            for p in range(2):
                for d in range(NT):
                    both = []
                    for half in range(2):
                        lane = 64 * half + 32 * (i % 2) + 16 * p + d
                        value = raw[pl.ds(8 * half * ROWS + 32 * i + 16 * p + d, 8, stride=ROWS), :]
                        both.append(live * (value - jnp.broadcast_to(mode[:, lane:lane + 1], (8, CH))))
                    send[i, d, p] = jnp.concatenate(both, axis=0).astype(jnp.bfloat16)
        for s in range(1, NT):
            remote(
                send.at[first:last, (tm + s) % NT], band.at[first:last, tm],
                re_send.at[group], re_recv.at[group], at_t(s),
            ).start()
        for i in range(first, last):
            band[i, tm] = send[i, tm]

    def whiten(i):
        real = band[i, :, 0].reshape(BLOCKS, CH).astype(jnp.float32)
        imag = band[i, :, 1].reshape(BLOCKS, CH).astype(jnp.float32)
        power = jnp.sum(real * real + imag * imag, axis=0, keepdims=True) / BLOCKS
        scale = lax.rsqrt(power + EPS)
        real, imag = real * scale, imag * scale
        mats[i, 0:BLOCKS, 0:CH] = real.astype(jnp.bfloat16)
        mats[i, BLOCKS:, 0:CH] = imag.astype(jnp.bfloat16)
        mats[i, 0:BLOCKS, CH:] = imag.astype(jnp.bfloat16)
        mats[i, BLOCKS:, CH:] = (-real).astype(jnp.bfloat16)
        rows = dot_nt(sel_ref[...], mats[i, :, 0:CH]).astype(jnp.bfloat16)
        for h in range(2):
            kind, u = UNITS[(i, h)]
            piece = rows[HALF * h:HALF * (h + 1)]
            if kind == 1:
                g1[u, z, 0] = piece
            else:
                g2[u, y, z] = piece

    def first_y(u, stage):
        if stage == 0:
            mine = g1.at[u, z, 0]
            start((Y1, u), mine, g1.at[u, z, 3], s1.at[u, 0], r1.at[u, 0], at_y(1))
            start((Y1, u), mine, g1.at[u, z, 1], s1.at[u, 1], r1.at[u, 1], at_y(-1))
        else:
            arrived(g1.at[u, z, 3], r1.at[u, 0])
            arrived(g1.at[u, z, 1], r1.at[u, 1])
            if u % 2 == 0:
                start((Y1, u), g1.at[u, z, 3], g1.at[u, z, 2], s1.at[u, 2], r1.at[u, 2], at_y(1))
            else:
                start((Y1, u), g1.at[u, z, 1], g1.at[u, z, 2], s1.at[u, 2], r1.at[u, 2], at_y(-1))

    def own_z(u, stage):
        left, right = (z - stage + NZ) % NZ, (z + stage) % NZ
        if 0 < stage < 4:
            arrived(g1.at[u, left, 0], r1.at[u, 9 + 2 * stage])
            arrived(g1.at[u, right, 0], r1.at[u, 10 + 2 * stage])
        if stage == 4:
            arrived(g1.at[u, left, 0], r1.at[u, 17])
            return
        a, b = g1.at[u, left, 0], g1.at[u, right, 0]
        if stage < 3 or u % 2 == 1:
            to = 17 if stage == 3 else 11 + 2 * stage
            start((OWN1, u), a, a, s1.at[u, to], r1.at[u, to], at_z(1))
        if stage < 3 or u % 2 == 0:
            to = 17 if stage == 3 else 12 + 2 * stage
            start((OWN1, u), b, b, s1.at[u, to], r1.at[u, to], at_z(-1))

    def then_z(u, stage):
        low = 1 if u in EARLY else 0
        middle = 2 if low == 0 or u % 2 == 1 else 3
        left, right = (z - stage + NZ) % NZ, (z + stage) % NZ
        if stage == 0:
            arrived(g1.at[u, z, 2], r1.at[u, 2])
        elif stage < 4:
            arrived(g1.at[u, left, low:4], r1.at[u, 1 + 2 * stage])
            arrived(g1.at[u, right, low:4], r1.at[u, 2 + 2 * stage])
        else:
            arrived(g1.at[u, left, low:middle], r1.at[u, 9])
            arrived(g1.at[u, left, middle:4], r1.at[u, 10])
            if low:
                own_z(u, 4)
            lines(u, (4,))
            return
        if stage < 3:
            a, b = g1.at[u, left, low:4], g1.at[u, right, low:4]
        else:
            a, b = g1.at[u, left, low:middle], g1.at[u, right, middle:4]
        start((Z1, u, stage == 3), a, a, s1.at[u, 3 + 2 * stage], r1.at[u, 3 + 2 * stage], at_z(1))
        start((Z1, u, stage == 3), b, b, s1.at[u, 4 + 2 * stage], r1.at[u, 4 + 2 * stage], at_z(-1))
        if stage == 3:
            for steps in ((-3, -2, -1, 0), (1, 2, 3)):
                lines(u, steps)
            for key in ((Y1, u), (OWN1, u), (Z1, u, False)):
                settle(key)

    def lines(u, steps):
        i, h = PLACE[(1, u)]
        at = [(z + step + NZ) % NZ for step in steps]
        left = jnp.concatenate([g1[u, zz].reshape(NY * HALF, 2 * BLOCKS) for zz in at], axis=0)
        both = jnp.dot(left, mats[i], preferred_element_type=jnp.float32) * (1.0 / BLOCKS)
        both = both.astype(jnp.bfloat16).reshape(len(steps), NY, HALF, 2 * CH)
        for k, zz in enumerate(at):
            for up in range(NY):
                out_ref[0, i, (y + up) % NY, zz, h] = both[k, up, :, 0:CH]
                out_ref[1, i, (y + up) % NY, zz, h] = both[k, up, :, CH:]

    def first_z(u, stage):
        left, right = (z - stage + NZ) % NZ, (z + stage) % NZ
        if stage > 0:
            arrived(g2.at[u, y, left], r2.at[u, 2 * stage - 2])
            arrived(g2.at[u, y, right], r2.at[u, 2 * stage - 1])
        a, b = g2.at[u, y, left], g2.at[u, y, right]
        if stage < 3 or u % 2 == 0:
            start((Z2, u), a, a, s2.at[u, 2 * stage], r2.at[u, 2 * stage], at_z(1))
        if stage < 3 or u % 2 == 1:
            start((Z2, u), b, b, s2.at[u, 2 * stage + 1], r2.at[u, 2 * stage + 1], at_z(-1))

    def then_y(u, stage):
        down, up, far = (y - 1 + NY) % NY, (y + 1) % NY, (y + 2) % NY
        if stage == 0:
            arrived(g2.at[u, y, (z + 4) % NZ], r2.at[u, 6 + u % 2])
            start((Y2, u, 0), g2.at[u, y], g2.at[u, y], s2.at[u, 8], r2.at[u, 8], at_y(1))
            start((Y2, u, 0), g2.at[u, y], g2.at[u, y], s2.at[u, 9], r2.at[u, 9], at_y(-1))
        elif stage == 1:
            arrived(g2.at[u, down], r2.at[u, 8])
            arrived(g2.at[u, up], r2.at[u, 9])
            a, b = g2.at[u, down, 0:4], g2.at[u, up, 4:8]
            start((Y2, u, 1), a, a, s2.at[u, 10], r2.at[u, 10], at_y(1))
            start((Y2, u, 1), b, b, s2.at[u, 11], r2.at[u, 11], at_y(-1))
            columns(u, (-1, 0, 1))
            settle((Z2, u))
        else:
            arrived(g2.at[u, far, 0:4], r2.at[u, 10])
            arrived(g2.at[u, far, 4:8], r2.at[u, 11])
            columns(u, (2,))
            settle((Y2, u, 0))

    def columns(u, steps):
        i, h = PLACE[(2, u)]
        at = [(y + step + NY) % NY for step in steps]
        left = jnp.concatenate([g2[u, yy].reshape(NZ * HALF, 2 * BLOCKS) for yy in at], axis=0)
        both = jnp.dot(left, mats[i], preferred_element_type=jnp.float32) * (1.0 / BLOCKS)
        both = both.astype(jnp.bfloat16).reshape(len(steps), NZ, HALF, 2 * CH)
        for k, yy in enumerate(at):
            out_ref[0, i, yy, :, h] = both[k, :, :, 0:CH]
            out_ref[1, i, yy, :, h] = both[k, :, :, CH:]

    def take(group):
        first, last = GROUPS[group]
        arrived(band.at[first:last, 0:NT - 1], re_recv.at[group])
        for i in range(first, last):
            whiten(i)

    def free(group):
        first, last = GROUPS[group]
        arrived(send.at[first:last, 0:NT - 1], re_send.at[group])

    steps = (take, first_y, then_z, own_z, first_z, then_y)
    close_sum(0)
    give(0)
    close_sum(1)
    give(1)
    for at, (step, unit, stage) in enumerate(ORDER):
        if at == LATE:
            give(2)
        if at == LATE + 44:
            settle("sum")
            for group in range(len(GROUPS)):
                free(group)
        if step == TAKE:
            take(unit)
        else:
            steps[step](unit, stage)
    for key in list(sent):
        settle(key)


def body(strain_record, dead_channels, source_channels, band_start):
    vmem = pl.BlockSpec(memory_space=pltpu.VMEM)
    hbm = pl.BlockSpec(memory_space=pltpu.HBM)
    dma = pltpu.SemaphoreType.DMA
    out = pl.pallas_call(
        kernel,
        out_shape=jax.ShapeDtypeStruct((2, FQ, NY, NZ, 2, HALF, CH), jnp.bfloat16),
        in_specs=[hbm] * 4 + [pl.BlockSpec(memory_space=pltpu.SMEM)],
        out_specs=vmem,
        scratch_shapes=[
            pltpu.VMEM((CH, NT * NFFT), jnp.bfloat16),
            pltpu.VMEM((2, FQ * NT, NFFT), jnp.float32),
            pltpu.SMEM((DEAD,), jnp.int32),
            pltpu.SMEM((SRC,), jnp.int32),
            pltpu.VMEM((PAD, NFFT), jnp.bfloat16),
            pltpu.VMEM((SRC, CH), jnp.bfloat16),
            pltpu.VMEM((NT, CH, PAD), jnp.float32),
            pltpu.VMEM((NT * ROWS, CH), jnp.float32),
            pltpu.VMEM((NT, PAD), jnp.float32),
            pltpu.VMEM((3, 8, CH), jnp.float32),
            pltpu.VMEM((NZ - 1, 3, 8, CH), jnp.float32),
            pltpu.VMEM((3, 8, CH), jnp.float32),
            pltpu.VMEM((NY - 1, 3, 8, CH), jnp.float32),
            pltpu.VMEM((3, 8, CH), jnp.float32),
            pltpu.VMEM((FQ, NT, 2, NT, CH), jnp.bfloat16),
            pltpu.VMEM((FQ, NT, 2, NT, CH), jnp.bfloat16),
            pltpu.VMEM((FQ, 2 * BLOCKS, 2 * CH), jnp.bfloat16),
            pltpu.VMEM((NP1, NZ, NY, HALF, 2 * BLOCKS), jnp.bfloat16),
            pltpu.VMEM((NP2, NY, NZ, HALF, 2 * BLOCKS), jnp.bfloat16),
            dma((7,)), dma((2, 10)), dma((2, 10)), dma((3,)), dma((3,)),
            dma((NP1, 18)), dma((NP1, 18)), dma((NP2, 12)), dma((NP2, 12)),
        ],
        compiler_params=pltpu.CompilerParams(
            collective_id=0, has_side_effects=True, vmem_limit_bytes=48 * 1024 * 1024
        ),
    )(*[
        pltpu.with_memory_space_constraint(array, pltpu.HBM)
        for array in (strain_record, jnp.asarray(fixed_tables()), dead_channels, source_channels)
    ], band_start)
    return out.reshape(2, FQ, NY * NZ * SRC, CH)


def solution(mesh):
    in_specs = (P("chan", "tm"), P(), P("chan"), P())
    out_specs = P(None, "tm", None, "chan")
    return jax.shard_map(body, mesh=mesh, in_specs=in_specs, out_specs=out_specs, check_vma=False)
```

time: 324 us -> 81.4 us (0.25)
  the two profiles are of different devices: /device:TPU:8 before, /device:TPU:14 now
where the time goes in v1:
time: 81.4 us; the launch traced here: 81.2 us
  Pallas kernels  79.1 us (97%)
  local copies, waits for them, and re-layouts  1.49 us (2%)
    pallas_call x1, Pallas kernels, body(): pl.pallas_call(kernel, out_shape=jax.ShapeDtypeStruct((2, FQ, NY, NZ, 2,...  79.1 us

profile of v1, /device:TPU:14, one launch (start us, length us, event | category | flops | bytes accessed | tf_op | source)
XLA Modules:
  0.0 81.2 jit_solution(6916976609035961769)
XLA Ops:
  0.7 79.1 %shard_map.55 = bf16[2,5,4,8,2,16,128]{6,5,4,3,2,1,0:T(8,128)(2,1)S(1)} custom-call(bf16[128,8192]{1,0:T(8,128)(2,1)} %x_hbm.1, f32[2,80,512]{2,1,0:T(8,128)} %constant.2.clone.fixed_hbm, s32[200]{0:T(256)} %dead_hbm.1, s32[32]{0:T(128)} %source_hbm.1, s32[1]{0:T(128)S(6)} %copy.7.start_ref), custom_call_target="tpu_custom_call" | custom-call | tf_op jit(solution)/shard_map/pallas_call | solution.py:373
  79.7 1.5 %copy.8 = bf16[2,5,1024,128]{3,2,1,0:T(8,128)(2,1)} copy(bf16[2,5,1024,128]{3,2,1,0:T(8,128)(2,1)S(1)} %bitcast.1) | data formatting | bytes 5242880

commit v2 on v1

--- a/solution.py
+++ b/solution.py
@@ -19,6 +19,7 @@
 ROWS = 2 * FQ * NT
 PAD = 256
 EPS = 1e-06
+FAR_FIRST = (4, 3, 5, 12, 11, 13, 2, 6, 10, 14, 8, 7, 9, 1, 15)
 NP1, NP2 = 7, 3
 
 UNITS = {(0, 0): (2, 0), (0, 1): (1, 0), (1, 0): (2, 1), (1, 1): (1, 1), (2, 0): (2, 2), (2, 1): (1, 2), (3, 0): (1, 3), (3, 1): (1, 4), (4, 0): (1, 5), (4, 1): (1, 6)}
@@ -55,21 +56,27 @@
 
 def kernel(
     x_hbm, fixed_hbm, dead_hbm, source_hbm, start_ref, out_ref,
-    x_ref, fixed, dead_ref, source_ref, table_ref, sel_ref, spec, raw, sums,
+    x_ref, fixed, dead_ref, source_ref, table_ref, sel_ref, raw, sums,
     part, parts_in, line, lines_in, common, send, band, mats, g1, g2,
     in_sem, ps_send, ps_recv, re_send, re_recv, s1, r1, s2, r2,
 ):
     chan, tm = lax.axis_index("chan"), lax.axis_index("tm")
-    y, z = chan // NZ, chan % NZ
+    y, z = lax.div(chan, NZ), lax.rem(chan, NZ)
+
+    ys = [lax.rem(y + step, NY) for step in range(NY)]
+    zs = [lax.rem(z + step, NZ) for step in range(NZ)]
+    ts = [lax.rem(tm + step, NT) for step in range(NT)]
+    along_y = [(ys[step] * NZ + z, tm) for step in range(NY)]
+    along_z = [(y * NZ + zs[step], tm) for step in range(NZ)]
 
     def at_y(step):
-        return {"chan": (y + step + NY) % NY * NZ + z}
+        return along_y[step % NY]
 
     def at_z(step):
-        return {"chan": y * NZ + (z + step + NZ) % NZ}
+        return along_z[step % NZ]
 
     def at_t(step):
-        return {"tm": (tm + step) % NT}
+        return (chan, ts[step % NT])
 
     def remote(src, dst, send_sem, recv_sem, where):
         return pltpu.make_async_remote_copy(
@@ -125,68 +132,71 @@
     live = lax.fori_loop(0, DEAD // 8, strike, jnp.ones((8, CH), jnp.float32))
     live_rows = jnp.broadcast_to(live[0:1], (CH, CH)).T
     live_rows = jnp.concatenate([live_rows, live_rows], axis=1)
+    fetches[2].wait()
+    for i in range(FQ):
+        cos_i, sin_i = fixed[0, NT * i:NT * (i + 1)], fixed[1, NT * i:NT * (i + 1)]
+        table_ref[32 * i:32 * i + 16] = (shift_cos * cos_i - shift_sin * sin_i).astype(jnp.bfloat16)
+        table_ref[32 * i + 16:32 * i + 32] = (-(shift_sin * cos_i + shift_cos * sin_i)).astype(jnp.bfloat16)
+    table_ref[ROWS:] = jnp.zeros((PAD - ROWS, NFFT), jnp.bfloat16)
+
+    for k in range(4):
+        fetches[3 + k].wait()
+        blocks = [x_ref[:, (4 * k + b) * NFFT:(4 * k + b + 1) * NFFT] for b in range(4)]
+        values = dot_nt(jnp.concatenate(blocks, axis=0), table_ref[...])
+        for b in range(4):
+            value = values[CH * b:CH * (b + 1)]
+            sums[4 * k + b:4 * k + b + 1] = jnp.sum(value * live_rows, axis=0, keepdims=True)
+    for q in range(3):
+        lanes = slice(64 * q, 64 * q + 64)
+        part[q] = jnp.concatenate([sums[0:8, lanes], sums[8:16, lanes]], axis=1)
+
+    pl.semaphore_wait(barrier, (NZ - 1) + (NY - 1) + (NT - 1))
+
+    pieces = (slice(0, 1), slice(1, 3))
+
+    def sum_z(n):
+        for s in range(1, NZ):
+            start(
+                "sum", part.at[pieces[n]], parts_in.at[s - 1, pieces[n]],
+                ps_send.at[n, s - 1], ps_recv.at[n, s - 1], at_z(s),
+            )
+
+    def sum_y(n):
+        total = part[pieces[n]]
+        for s in range(1, NZ):
+            arrived(parts_in.at[s - 1, pieces[n]], ps_recv.at[n, s - 1])
+            total = total + parts_in[s - 1, pieces[n]]
+        line[pieces[n]] = total
+        for s in range(1, NY):
+            start(
+                "sum", line.at[pieces[n]], lines_in.at[s - 1, pieces[n]],
+                ps_send.at[n, 6 + s], ps_recv.at[n, 6 + s], at_y(s),
+            )
+
+    def close_sum(n):
+        total = line[pieces[n]]
+        for s in range(1, NY):
+            arrived(lines_in.at[s - 1, pieces[n]], ps_recv.at[n, 6 + s])
+            total = total + lines_in[s - 1, pieces[n]]
+        common[pieces[n]] = total / (NCHAN - DEAD)
+
+    def transform(b, carry):
+        samples = x_ref[:, pl.ds(pl.multiple_of(b * NFFT, NFFT), NFFT)]
+        raw[pl.ds(b, ROWS, stride=NT), :] = dot_nt(table_ref[0:ROWS], samples)
+        return carry
+
+    sum_z(0)
+    sum_z(1)
     source_ids = chan * CH + lax.broadcasted_iota(jnp.int32, (SRC, CH), 1)
     source_rows = lax.broadcasted_iota(jnp.int32, (SRC, CH), 0)
     wanted = jnp.zeros((SRC, CH), jnp.int32)
     for k in range(SRC):
         wanted = jnp.where(source_rows == k, source_ref[k], wanted)
     sel_ref[...] = jnp.where(wanted == source_ids, 1.0, 0.0).astype(jnp.bfloat16)
-    fetches[2].wait()
-    for i in range(FQ):
-        cos_i, sin_i = fixed[0, NT * i:NT * (i + 1)], fixed[1, NT * i:NT * (i + 1)]
-        table_ref[32 * i:32 * i + 16] = (shift_cos * cos_i - shift_sin * sin_i).astype(jnp.bfloat16)
-        table_ref[32 * i + 16:32 * i + 32] = (-(shift_sin * cos_i + shift_cos * sin_i)).astype(jnp.bfloat16)
-    table_ref[ROWS:] = jnp.zeros((PAD - ROWS, NFFT), jnp.bfloat16)
-
-    for k in range(4):
-        fetches[3 + k].wait()
-        blocks = [x_ref[:, (4 * k + b) * NFFT:(4 * k + b + 1) * NFFT] for b in range(4)]
-        values = dot_nt(jnp.concatenate(blocks, axis=0), table_ref[...])
-        for b in range(4):
-            value = values[CH * b:CH * (b + 1)]
-            spec[4 * k + b] = value
-            sums[4 * k + b:4 * k + b + 1] = jnp.sum(value * live_rows, axis=0, keepdims=True)
-    for q in range(3):
-        lanes = slice(64 * q, 64 * q + 64)
-        part[q] = jnp.concatenate([sums[0:8, lanes], sums[8:16, lanes]], axis=1)
-
-    pl.semaphore_wait(barrier, (NZ - 1) + (NY - 1) + (NT - 1))
-
-    pieces = (slice(0, 1), slice(1, 3))
-    for n, piece in enumerate(pieces):
-        for s in range(1, NZ):
-            start(
-                "sum", part.at[piece], parts_in.at[s - 1, piece],
-                ps_send.at[n, s - 1], ps_recv.at[n, s - 1], at_z(s),
-            )
-
-    def turn(b, carry):
-        to = pl.multiple_of(b * ROWS, ROWS)
-        raw[pl.ds(to, CH), :] = spec[b, :, 0:CH].T
-        raw[pl.ds(to + CH, ROWS - CH), :] = spec[b, :, CH:].T[0:ROWS - CH]
-        return carry
-
-    lax.fori_loop(0, NT // 2, turn, 0)
-    for n, piece in enumerate(pieces):
-        total = part[piece]
-        for s in range(1, NZ):
-            arrived(parts_in.at[s - 1, piece], ps_recv.at[n, s - 1])
-            total = total + parts_in[s - 1, piece]
-        line[piece] = total
-        for s in range(1, NY):
-            start(
-                "sum", line.at[piece], lines_in.at[s - 1, piece],
-                ps_send.at[n, 6 + s], ps_recv.at[n, 6 + s], at_y(s),
-            )
-    lax.fori_loop(NT // 2, NT, turn, 0)
-
-    def close_sum(n):
-        piece = pieces[n]
-        total = line[piece]
-        for s in range(1, NY):
-            arrived(lines_in.at[s - 1, piece], ps_recv.at[n, 6 + s])
-            total = total + lines_in[s - 1, piece]
-        common[piece] = total / (NCHAN - DEAD)
+    lax.fori_loop(0, NT // 2, transform, 0)
+    sum_y(0)
+    sum_y(1)
+    lax.fori_loop(NT // 2, NT, transform, 0)
 
     def give(group):
         first, last = GROUPS[group]
@@ -197,12 +207,13 @@
                     both = []
                     for half in range(2):
                         lane = 64 * half + 32 * (i % 2) + 16 * p + d
-                        value = raw[pl.ds(8 * half * ROWS + 32 * i + 16 * p + d, 8, stride=ROWS), :]
+                        row = NT * (32 * i + 16 * p + d) + 8 * half
+                        value = raw[row:row + 8]
                         both.append(live * (value - jnp.broadcast_to(mode[:, lane:lane + 1], (8, CH))))
                     send[i, d, p] = jnp.concatenate(both, axis=0).astype(jnp.bfloat16)
-        for s in range(1, NT):
+        for s in FAR_FIRST:
             remote(
-                send.at[first:last, (tm + s) % NT], band.at[first:last, tm],
+                send.at[first:last, ts[s]], band.at[first:last, tm],
                 re_send.at[group], re_recv.at[group], at_t(s),
             ).start()
         for i in range(first, last):
@@ -241,7 +252,7 @@
                 start((Y1, u), g1.at[u, z, 1], g1.at[u, z, 2], s1.at[u, 2], r1.at[u, 2], at_y(-1))
 
     def own_z(u, stage):
-        left, right = (z - stage + NZ) % NZ, (z + stage) % NZ
+        left, right = zs[-stage % NZ], zs[stage]
         if 0 < stage < 4:
             arrived(g1.at[u, left, 0], r1.at[u, 9 + 2 * stage])
             arrived(g1.at[u, right, 0], r1.at[u, 10 + 2 * stage])
@@ -259,7 +270,7 @@
     def then_z(u, stage):
         low = 1 if u in EARLY else 0
         middle = 2 if low == 0 or u % 2 == 1 else 3
-        left, right = (z - stage + NZ) % NZ, (z + stage) % NZ
+        left, right = zs[-stage % NZ], zs[stage]
         if stage == 0:
             arrived(g1.at[u, z, 2], r1.at[u, 2])
         elif stage < 4:
@@ -286,17 +297,17 @@
 
     def lines(u, steps):
         i, h = PLACE[(1, u)]
-        at = [(z + step + NZ) % NZ for step in steps]
+        at = [zs[step % NZ] for step in steps]
         left = jnp.concatenate([g1[u, zz].reshape(NY * HALF, 2 * BLOCKS) for zz in at], axis=0)
         both = jnp.dot(left, mats[i], preferred_element_type=jnp.float32) * (1.0 / BLOCKS)
         both = both.astype(jnp.bfloat16).reshape(len(steps), NY, HALF, 2 * CH)
         for k, zz in enumerate(at):
             for up in range(NY):
-                out_ref[0, i, (y + up) % NY, zz, h] = both[k, up, :, 0:CH]
-                out_ref[1, i, (y + up) % NY, zz, h] = both[k, up, :, CH:]
+                out_ref[0, i, ys[up], zz, h] = both[k, up, :, 0:CH]
+                out_ref[1, i, ys[up], zz, h] = both[k, up, :, CH:]
 
     def first_z(u, stage):
-        left, right = (z - stage + NZ) % NZ, (z + stage) % NZ
+        left, right = zs[-stage % NZ], zs[stage]
         if stage > 0:
             arrived(g2.at[u, y, left], r2.at[u, 2 * stage - 2])
             arrived(g2.at[u, y, right], r2.at[u, 2 * stage - 1])
@@ -307,9 +318,9 @@
             start((Z2, u), b, b, s2.at[u, 2 * stage + 1], r2.at[u, 2 * stage + 1], at_z(-1))
 
     def then_y(u, stage):
-        down, up, far = (y - 1 + NY) % NY, (y + 1) % NY, (y + 2) % NY
+        down, up, far = ys[3], ys[1], ys[2]
         if stage == 0:
-            arrived(g2.at[u, y, (z + 4) % NZ], r2.at[u, 6 + u % 2])
+            arrived(g2.at[u, y, zs[4]], r2.at[u, 6 + u % 2])
             start((Y2, u, 0), g2.at[u, y], g2.at[u, y], s2.at[u, 8], r2.at[u, 8], at_y(1))
             start((Y2, u, 0), g2.at[u, y], g2.at[u, y], s2.at[u, 9], r2.at[u, 9], at_y(-1))
         elif stage == 1:
@@ -328,7 +339,7 @@
 
     def columns(u, steps):
         i, h = PLACE[(2, u)]
-        at = [(y + step + NY) % NY for step in steps]
+        at = [ys[step % NY] for step in steps]
         left = jnp.concatenate([g2[u, yy].reshape(NZ * HALF, 2 * BLOCKS) for yy in at], axis=0)
         both = jnp.dot(left, mats[i], preferred_element_type=jnp.float32) * (1.0 / BLOCKS)
         both = both.astype(jnp.bfloat16).reshape(len(steps), NZ, HALF, 2 * CH)
@@ -382,7 +393,6 @@
             pltpu.SMEM((SRC,), jnp.int32),
             pltpu.VMEM((PAD, NFFT), jnp.bfloat16),
             pltpu.VMEM((SRC, CH), jnp.bfloat16),
-            pltpu.VMEM((NT, CH, PAD), jnp.float32),
             pltpu.VMEM((NT * ROWS, CH), jnp.float32),
             pltpu.VMEM((NT, PAD), jnp.float32),
             pltpu.VMEM((3, 8, CH), jnp.float32),

time: 81.4 us -> 81.3 us (level)
  no operation moved by 1% of the time
where the time goes in v2:
time: 81.3 us; the launch traced here: 81.2 us
  Pallas kernels  79 us (97%)
  local copies, waits for them, and re-layouts  1.49 us (2%)
    pallas_call x1, Pallas kernels, body(): pl.pallas_call(kernel, out_shape=jax.ShapeDtypeStruct((2, FQ, NY, NZ, 2,...  79 us

profile of v2, /device:TPU:14, one launch (start us, length us, event | category | flops | bytes accessed | tf_op | source)
XLA Modules:
  0.0 81.2 jit_solution(10659919292231586030)
XLA Ops:
  0.7 79.0 %shard_map.55 = bf16[2,5,4,8,2,16,128]{6,5,4,3,2,1,0:T(8,128)(2,1)S(1)} custom-call(bf16[128,8192]{1,0:T(8,128)(2,1)} %x_hbm.1, f32[2,80,512]{2,1,0:T(8,128)} %constant.2.clone.fixed_hbm, s32[200]{0:T(256)} %dead_hbm.1, s32[32]{0:T(128)} %source_hbm.1, s32[1]{0:T(128)S(6)} %copy.7.start_ref), custom_call_target="tpu_custom_call" | custom-call | tf_op jit(solution)/shard_map/pallas_call | solution.py:384
  79.7 1.5 %copy.8 = bf16[2,5,1024,128]{3,2,1,0:T(8,128)(2,1)} copy(bf16[2,5,1024,128]{3,2,1,0:T(8,128)(2,1)S(1)} %bitcast.1) | data formatting | bytes 5242880

commit v3 on v2

--- a/solution.py
+++ b/solution.py
@@ -116,28 +116,21 @@
     ):
         pl.semaphore_signal(barrier, inc=1, device_id=peer, device_id_type=pl.DeviceIdType.MESH)
 
-    for k in range(2):
-        fetches[k].wait()
     phase = start_ref[0] * lax.broadcasted_iota(jnp.int32, (8, NFFT), 1) % NFFT
     angle = 2.0 * jnp.pi / NFFT * phase.astype(jnp.float32)
     shift_cos = jnp.concatenate([jnp.cos(angle)] * 2, axis=0)
     shift_sin = jnp.concatenate([jnp.sin(angle)] * 2, axis=0)
-    ids = chan * CH + lax.broadcasted_iota(jnp.int32, (8, CH), 1)
-
-    def strike(step, mask):
-        for k in range(8):
-            mask = jnp.where(ids == dead_ref[8 * step + k], 0.0, mask)
-        return mask
-
-    live = lax.fori_loop(0, DEAD // 8, strike, jnp.ones((8, CH), jnp.float32))
-    live_rows = jnp.broadcast_to(live[0:1], (CH, CH)).T
-    live_rows = jnp.concatenate([live_rows, live_rows], axis=1)
     fetches[2].wait()
     for i in range(FQ):
         cos_i, sin_i = fixed[0, NT * i:NT * (i + 1)], fixed[1, NT * i:NT * (i + 1)]
         table_ref[32 * i:32 * i + 16] = (shift_cos * cos_i - shift_sin * sin_i).astype(jnp.bfloat16)
         table_ref[32 * i + 16:32 * i + 32] = (-(shift_sin * cos_i + shift_cos * sin_i)).astype(jnp.bfloat16)
     table_ref[ROWS:] = jnp.zeros((PAD - ROWS, NFFT), jnp.bfloat16)
+
+    fetches[0].wait()
+    ids = chan * CH + lax.broadcasted_iota(jnp.int32, (CH, DEAD), 0)
+    struck = jnp.where(ids == jnp.broadcast_to(dead_ref[...][None, :], (CH, DEAD)), 1.0, 0.0)
+    live_rows = jnp.broadcast_to(1.0 - jnp.max(struck, axis=1, keepdims=True), (CH, PAD))
 
     for k in range(4):
         fetches[3 + k].wait()
@@ -187,6 +180,8 @@
 
     sum_z(0)
     sum_z(1)
+    live = live_rows[:, 0:CH].T[0:8]
+    fetches[1].wait()
     source_ids = chan * CH + lax.broadcasted_iota(jnp.int32, (SRC, CH), 1)
     source_rows = lax.broadcasted_iota(jnp.int32, (SRC, CH), 0)
     wanted = jnp.zeros((SRC, CH), jnp.int32)
@@ -244,25 +239,28 @@
             start((Y1, u), mine, g1.at[u, z, 3], s1.at[u, 0], r1.at[u, 0], at_y(1))
             start((Y1, u), mine, g1.at[u, z, 1], s1.at[u, 1], r1.at[u, 1], at_y(-1))
         else:
-            arrived(g1.at[u, z, 3], r1.at[u, 0])
-            arrived(g1.at[u, z, 1], r1.at[u, 1])
             if u % 2 == 0:
+                arrived(g1.at[u, z, 3], r1.at[u, 0])
                 start((Y1, u), g1.at[u, z, 3], g1.at[u, z, 2], s1.at[u, 2], r1.at[u, 2], at_y(1))
+                arrived(g1.at[u, z, 1], r1.at[u, 1])
             else:
+                arrived(g1.at[u, z, 1], r1.at[u, 1])
                 start((Y1, u), g1.at[u, z, 1], g1.at[u, z, 2], s1.at[u, 2], r1.at[u, 2], at_y(-1))
+                arrived(g1.at[u, z, 3], r1.at[u, 0])
 
     def own_z(u, stage):
         left, right = zs[-stage % NZ], zs[stage]
-        if 0 < stage < 4:
-            arrived(g1.at[u, left, 0], r1.at[u, 9 + 2 * stage])
-            arrived(g1.at[u, right, 0], r1.at[u, 10 + 2 * stage])
         if stage == 4:
             arrived(g1.at[u, left, 0], r1.at[u, 17])
             return
         a, b = g1.at[u, left, 0], g1.at[u, right, 0]
+        if stage > 0:
+            arrived(a, r1.at[u, 9 + 2 * stage])
         if stage < 3 or u % 2 == 1:
             to = 17 if stage == 3 else 11 + 2 * stage
             start((OWN1, u), a, a, s1.at[u, to], r1.at[u, to], at_z(1))
+        if stage > 0:
+            arrived(b, r1.at[u, 10 + 2 * stage])
         if stage < 3 or u % 2 == 0:
             to = 17 if stage == 3 else 12 + 2 * stage
             start((OWN1, u), b, b, s1.at[u, to], r1.at[u, to], at_z(-1))
@@ -271,12 +269,7 @@
         low = 1 if u in EARLY else 0
         middle = 2 if low == 0 or u % 2 == 1 else 3
         left, right = zs[-stage % NZ], zs[stage]
-        if stage == 0:
-            arrived(g1.at[u, z, 2], r1.at[u, 2])
-        elif stage < 4:
-            arrived(g1.at[u, left, low:4], r1.at[u, 1 + 2 * stage])
-            arrived(g1.at[u, right, low:4], r1.at[u, 2 + 2 * stage])
-        else:
+        if stage == 4:
             arrived(g1.at[u, left, low:middle], r1.at[u, 9])
             arrived(g1.at[u, left, middle:4], r1.at[u, 10])
             if low:
@@ -287,7 +280,13 @@
             a, b = g1.at[u, left, low:4], g1.at[u, right, low:4]
         else:
             a, b = g1.at[u, left, low:middle], g1.at[u, right, middle:4]
+        if stage == 0:
+            arrived(g1.at[u, z, 2], r1.at[u, 2])
+        else:
+            arrived(g1.at[u, left, low:4], r1.at[u, 1 + 2 * stage])
         start((Z1, u, stage == 3), a, a, s1.at[u, 3 + 2 * stage], r1.at[u, 3 + 2 * stage], at_z(1))
+        if stage > 0:
+            arrived(g1.at[u, right, low:4], r1.at[u, 2 + 2 * stage])
         start((Z1, u, stage == 3), b, b, s1.at[u, 4 + 2 * stage], r1.at[u, 4 + 2 * stage], at_z(-1))
         if stage == 3:
             for steps in ((-3, -2, -1, 0), (1, 2, 3)):
@@ -308,12 +307,13 @@
 
     def first_z(u, stage):
         left, right = zs[-stage % NZ], zs[stage]
+        a, b = g2.at[u, y, left], g2.at[u, y, right]
         if stage > 0:
-            arrived(g2.at[u, y, left], r2.at[u, 2 * stage - 2])
-            arrived(g2.at[u, y, right], r2.at[u, 2 * stage - 1])
-        a, b = g2.at[u, y, left], g2.at[u, y, right]
+            arrived(a, r2.at[u, 2 * stage - 2])
         if stage < 3 or u % 2 == 0:
             start((Z2, u), a, a, s2.at[u, 2 * stage], r2.at[u, 2 * stage], at_z(1))
+        if stage > 0:
+            arrived(b, r2.at[u, 2 * stage - 1])
         if stage < 3 or u % 2 == 1:
             start((Z2, u), b, b, s2.at[u, 2 * stage + 1], r2.at[u, 2 * stage + 1], at_z(-1))
 
@@ -324,10 +324,10 @@
             start((Y2, u, 0), g2.at[u, y], g2.at[u, y], s2.at[u, 8], r2.at[u, 8], at_y(1))
             start((Y2, u, 0), g2.at[u, y], g2.at[u, y], s2.at[u, 9], r2.at[u, 9], at_y(-1))
         elif stage == 1:
+            a, b = g2.at[u, down, 0:4], g2.at[u, up, 4:8]
             arrived(g2.at[u, down], r2.at[u, 8])
+            start((Y2, u, 1), a, a, s2.at[u, 10], r2.at[u, 10], at_y(1))
             arrived(g2.at[u, up], r2.at[u, 9])
-            a, b = g2.at[u, down, 0:4], g2.at[u, up, 4:8]
-            start((Y2, u, 1), a, a, s2.at[u, 10], r2.at[u, 10], at_y(1))
             start((Y2, u, 1), b, b, s2.at[u, 11], r2.at[u, 11], at_y(-1))
             columns(u, (-1, 0, 1))
             settle((Z2, u))
@@ -389,7 +389,7 @@
         scratch_shapes=[
             pltpu.VMEM((CH, NT * NFFT), jnp.bfloat16),
             pltpu.VMEM((2, FQ * NT, NFFT), jnp.float32),
-            pltpu.SMEM((DEAD,), jnp.int32),
+            pltpu.VMEM((DEAD,), jnp.int32),
             pltpu.SMEM((SRC,), jnp.int32),
             pltpu.VMEM((PAD, NFFT), jnp.bfloat16),
             pltpu.VMEM((SRC, CH), jnp.bfloat16),

time: 81.3 us -> 81.1 us (level)
  the two profiles are of different devices: /device:TPU:14 before, /device:TPU:8 now
where the time goes in v3:
time: 81.1 us; the launch traced here: 81 us
  Pallas kernels  78.8 us (97%)
  local copies, waits for them, and re-layouts  1.49 us (2%)
    pallas_call x1, Pallas kernels, body(): pl.pallas_call(kernel, out_shape=jax.ShapeDtypeStruct((2, FQ, NY, NZ, 2,...  78.8 us

profile of v3, /device:TPU:8, one launch (start us, length us, event | category | flops | bytes accessed | tf_op | source)
XLA Modules:
  0.0 81.0 jit_solution(16744904337860509496)
XLA Ops:
  0.7 78.8 %shard_map.55 = bf16[2,5,4,8,2,16,128]{6,5,4,3,2,1,0:T(8,128)(2,1)S(1)} custom-call(bf16[128,8192]{1,0:T(8,128)(2,1)} %x_hbm.1, f32[2,80,512]{2,1,0:T(8,128)} %constant.2.clone.fixed_hbm, s32[200]{0:T(256)} %dead_hbm.1, s32[32]{0:T(128)} %source_hbm.1, s32[1]{0:T(128)S(6)} %copy.7.start_ref), custom_call_target="tpu_custom_call" | custom-call | tf_op jit(solution)/shard_map/pallas_call | solution.py:384
  79.5 1.5 %copy.8 = bf16[2,5,1024,128]{3,2,1,0:T(8,128)(2,1)} copy(bf16[2,5,1024,128]{3,2,1,0:T(8,128)(2,1)S(1)} %bitcast.1) | data formatting | bytes 5242880

commit v4 on v3

--- a/solution.py
+++ b/solution.py
@@ -188,10 +188,11 @@
     for k in range(SRC):
         wanted = jnp.where(source_rows == k, source_ref[k], wanted)
     sel_ref[...] = jnp.where(wanted == source_ids, 1.0, 0.0).astype(jnp.bfloat16)
-    lax.fori_loop(0, NT // 2, transform, 0)
+    lax.fori_loop(0, 8, transform, 0, unroll=4)
     sum_y(0)
+    lax.fori_loop(8, 12, transform, 0, unroll=4)
     sum_y(1)
-    lax.fori_loop(NT // 2, NT, transform, 0)
+    lax.fori_loop(12, NT, transform, 0, unroll=4)
 
     def give(group):
         first, last = GROUPS[group]
@@ -289,8 +290,7 @@
             arrived(g1.at[u, right, low:4], r1.at[u, 2 + 2 * stage])
         start((Z1, u, stage == 3), b, b, s1.at[u, 4 + 2 * stage], r1.at[u, 4 + 2 * stage], at_z(-1))
         if stage == 3:
-            for steps in ((-3, -2, -1, 0), (1, 2, 3)):
-                lines(u, steps)
+            lines(u, (-3, -2, -1, 0, 1, 2, 3))
             for key in ((Y1, u), (OWN1, u), (Z1, u, False)):
                 settle(key)
 

time: 81.1 us -> 81.8 us (level)
  no operation moved by 1% of the time
where the time goes in v4:
time: 81.8 us; the launch traced here: 81.6 us
  Pallas kernels  79.5 us (97%)
  local copies, waits for them, and re-layouts  1.49 us (2%)
    pallas_call x1, Pallas kernels, body(): pl.pallas_call(kernel, out_shape=jax.ShapeDtypeStruct((2, FQ, NY, NZ, 2,...  79.5 us

profile of v4, /device:TPU:8, one launch (start us, length us, event | category | flops | bytes accessed | tf_op | source)
XLA Modules:
  0.0 81.6 jit_solution(15212041262965873185)
XLA Ops:
  0.7 79.5 %shard_map.55 = bf16[2,5,4,8,2,16,128]{6,5,4,3,2,1,0:T(8,128)(2,1)S(1)} custom-call(bf16[128,8192]{1,0:T(8,128)(2,1)} %x_hbm.1, f32[2,80,512]{2,1,0:T(8,128)} %constant.2.clone.fixed_hbm, s32[200]{0:T(256)} %dead_hbm.1, s32[32]{0:T(128)} %source_hbm.1, s32[1]{0:T(128)S(6)} %copy.7.start_ref), custom_call_target="tpu_custom_call" | custom-call | tf_op jit(solution)/shard_map/pallas_call | solution.py:384
  80.1 1.5 %copy.8 = bf16[2,5,1024,128]{3,2,1,0:T(8,128)(2,1)} copy(bf16[2,5,1024,128]{3,2,1,0:T(8,128)(2,1)S(1)} %bitcast.1) | data formatting | bytes 5242880

commit v5 on v3

--- a/solution.py
+++ b/solution.py
@@ -35,10 +35,10 @@
     (OWN1, 0, 2), (Z1, 0, 0), (Z2, 0, 2), (OWN1, 1, 2), (Z2, 1, 2), (Y1, 3, 1), (OWN1, 2, 2), (Z2, 2, 2),
     (Y1, 4, 1), (OWN1, 0, 3), (Y1, 5, 1), (Z1, 0, 1), (Y1, 6, 1), (Z2, 0, 3), (OWN1, 1, 3), (Z1, 1, 0), (Z1, 2, 0),
     (Z2, 1, 3), (OWN1, 2, 3), (Z1, 3, 0), (Z2, 2, 3), (Z1, 4, 0), (Z1, 5, 0), (Z1, 6, 0), (Z1, 0, 2), (Y2, 0, 0),
-    (Z1, 1, 1), (Y2, 1, 0), (Z1, 2, 1), (Z1, 3, 1), (Y2, 2, 0), (Z1, 4, 1), (Z1, 5, 1), (Y2, 0, 1), (Z1, 6, 1),
-    (Z1, 0, 3), (Z1, 1, 2), (Z1, 2, 2), (Z1, 3, 2), (Y2, 1, 1), (Z1, 4, 2), (Z1, 5, 2), (Z1, 6, 2), (Z1, 0, 4),
-    (Z1, 1, 3), (Y2, 2, 1), (Z1, 2, 3), (Z1, 3, 3), (Y2, 0, 2), (Z1, 4, 3), (Z1, 5, 3), (Y2, 1, 2), (Z1, 6, 3),
-    (Z1, 1, 4), (Z1, 2, 4), (Z1, 3, 4), (Y2, 2, 2), (Z1, 4, 4), (Z1, 5, 4), (Z1, 6, 4),
+    (Z1, 1, 1), (Y2, 1, 0), (Z1, 2, 1), (Z1, 3, 1), (Y2, 2, 0), (Z1, 4, 1), (Z1, 5, 1), (Z1, 6, 1), (Z1, 0, 3),
+    (Z1, 1, 2), (Z1, 2, 2), (Z1, 3, 2), (Z1, 4, 2), (Z1, 5, 2), (Z1, 6, 2), (Y2, 0, 1), (Z1, 0, 4), (Z1, 1, 3),
+    (Y2, 1, 1), (Z1, 2, 3), (Y2, 2, 1), (Z1, 3, 3), (Z1, 4, 3), (Z1, 5, 3), (Z1, 6, 3), (Z1, 1, 4), (Z1, 2, 4),
+    (Z1, 3, 4), (Z1, 4, 4), (Z1, 5, 4), (Z1, 6, 4), (Y2, 0, 2), (Y2, 1, 2), (Y2, 2, 2),
 )
 
 

time: 81.1 us -> 79.9 us (0.985)
  Pallas kernels: 78.8 us -> 77.6 us
    pallas_call x1, Pallas kernels: 78.8 us -> 77.6 us  [body(): pl.pallas_call(kernel, out_shape=jax.ShapeDtypeStruct((2, FQ, NY, NZ, 2,...]
where the time goes in v5:
time: 79.9 us; the launch traced here: 79.8 us
  Pallas kernels  77.6 us (97%)
  local copies, waits for them, and re-layouts  1.49 us (2%)
    pallas_call x1, Pallas kernels, body(): pl.pallas_call(kernel, out_shape=jax.ShapeDtypeStruct((2, FQ, NY, NZ, 2,...  77.6 us

profile of v5, /device:TPU:8, one launch (start us, length us, event | category | flops | bytes accessed | tf_op | source)
XLA Modules:
  0.0 79.8 jit_solution(10960266324879902424)
XLA Ops:
  0.7 77.6 %shard_map.55 = bf16[2,5,4,8,2,16,128]{6,5,4,3,2,1,0:T(8,128)(2,1)S(1)} custom-call(bf16[128,8192]{1,0:T(8,128)(2,1)} %x_hbm.1, f32[2,80,512]{2,1,0:T(8,128)} %constant.2.clone.fixed_hbm, s32[200]{0:T(256)} %dead_hbm.1, s32[32]{0:T(128)} %source_hbm.1, s32[1]{0:T(128)S(6)} %copy.7.start_ref), custom_call_target="tpu_custom_call" | custom-call | tf_op jit(solution)/shard_map/pallas_call | solution.py:384
  78.3 1.5 %copy.8 = bf16[2,5,1024,128]{3,2,1,0:T(8,128)(2,1)} copy(bf16[2,5,1024,128]{3,2,1,0:T(8,128)(2,1)S(1)} %bitcast.1) | data formatting | bytes 5242880
